TPU v7x, 256 devices: a whole 4x4x8 slice. The times are simulated.
256 devices in a mesh: tile: 64 (over y, z, core), head: 4 (over x).
Axes of the slice: x: 4, y: 4, z: 8, core: 2. Of those that a mesh axis runs over, the one named last changes fastest.
Arguments:
- tokens: bfloat16 [256, 262144], P('head', 'tile'), may hold values from -6 to 6
- grad_in: bfloat16 [256, 262144], P('head', 'tile'), may hold values from -6 to 6
- w_qkv: bfloat16 [3, 256, 256], P(None, 'head'), may hold values from -0.375 to 0.375
- w_out: bfloat16 [256, 256], P('head'), may hold values from -0.375 to 0.375
- neighbors: int32 [9, 262144], P(None, 'tile'), may hold values from 0 to 4479, as said below
- send_rows: int32 [64, 3, 128], P('tile'), may hold values from 0 to 4096, as said below
Outputs:
- d_tokens: float32 [256, 262144], P('head', 'tile')
- grad_qkv: float32 [3, 256, 256], P(None, 'head')
- grad_out: float32 [256, 256], P('head')
Inputs may be any that keep to these rules, and one draw needn't show every extreme that they name: `send_rows`: entries of list p of index d are rows of index d, live entries first, the rest equal to 4096; list 2 of every index is full, and list 0 of index 0 is half full. `neighbors`: slot 0 of row r of an index is r itself; an entry below 4096 lies within 64 rows of r, counted around the index's 4096 rows; every entry at or above 4096 points to a live entry of the list it names.
All inputs are finite; a program needn't handle non-finite values.
Results may differ from a plain program's by a relative error of at most 0.0059.
Values may be sent and summed in bfloat16 or wider, within the bound.
No kernel may reach another device: no remote copies, remote signals or barrier semaphores. Data moves between devices by JAX's collectives and lax.ppermute only.
A program may use at most 64 MiB of HBM per device.

v0:
```python
import math
import jax
import jax.numpy as jnp
from jax import lax
from jax.sharding import PartitionSpec as P

C = 256
HEADS = 8
NBR = 9


def passed_along(value, axis, steps):
    count = lax.axis_size(axis)
    pairs = [(source, (source + steps) % count) for source in range(count)]
    return lax.ppermute(value, axis, pairs)


def attention(extended, picks_all, query, grad_att, block_rows):
    channels = query.shape[0]
    row_count = query.shape[1]
    head_dim = C // HEADS
    local_heads = channels // head_dim
    score_scale = 1.0 / math.sqrt(head_dim)
    block_count = row_count // block_rows
    pick_blocks = picks_all.reshape(NBR, block_count, block_rows).transpose(1, 0, 2)
    query_blocks = query.reshape(channels, block_count, block_rows).transpose(1, 0, 2)
    dout_blocks = grad_att.reshape(channels, block_count, block_rows).transpose(1, 0, 2)

    def attend_block(totals, inputs):
        picks, query_rows, dout_rows = inputs
        near = extended[picks].astype(jnp.float32)
        near_keys = near[:, :, :channels].reshape(NBR, block_rows, local_heads, head_dim)
        near_values = near[:, :, channels:].reshape(NBR, block_rows, local_heads, head_dim)
        query_heads = query_rows.astype(jnp.float32).T.reshape(block_rows, local_heads, head_dim)
        dout_heads = dout_rows.T.reshape(block_rows, local_heads, head_dim)
        scores = jnp.einsum("rhd,jrhd->jrh", query_heads, near_keys) * score_scale
        expon = jnp.exp(scores)
        probs = expon / jnp.sum(expon, axis=0)
        attended = jnp.einsum("jrh,jrhd->rhd", probs, near_values)
        dprob = jnp.einsum("rhd,jrhd->jrh", dout_heads, near_values)
        dscore = probs * (dprob - jnp.sum(probs * dprob, axis=0))
        grad_query = jnp.einsum("jrh,jrhd->rhd", dscore, near_keys) * score_scale
        grad_keys = dscore[..., None] * query_heads[None] * score_scale
        grad_values = probs[..., None] * dout_heads[None]
        grad_near = jnp.concatenate(
            [
                grad_keys.reshape(NBR, block_rows, channels),
                grad_values.reshape(NBR, block_rows, channels),
            ],
            axis=2,
        )
        totals = totals.at[picks.reshape(-1)].add(grad_near.reshape(NBR * block_rows, 2 * channels))
        attended_cols = attended.reshape(block_rows, channels).astype(jnp.bfloat16).T
        query_cols = grad_query.reshape(block_rows, channels).T
        return (totals, (attended_cols, query_cols))

    start_grad = jnp.zeros((extended.shape[0], 2 * channels), jnp.float32)
    grad_ext, (attended, grad_query) = lax.scan(
        attend_block, start_grad, (pick_blocks, query_blocks, dout_blocks)
    )
    attended = attended.transpose(1, 0, 2).reshape(channels, row_count)
    grad_query = grad_query.transpose(1, 0, 2).reshape(channels, row_count)
    return (grad_ext, attended, grad_query)


def local(tokens, grad_in, w_qkv, w_out, neighbors, send_rows):
    groups = lax.axis_size("tile")
    border = send_rows.shape[2]
    offsets = (1, groups - 1, groups // 2)
    lists = send_rows[0]
    full_x, full_dy = (
        lax.all_gather(tokens, "head", axis=0, tiled=True),
        lax.all_gather(grad_in, "head", axis=0, tiled=True),
    )
    row_count = tokens.shape[1]
    channels = tokens.shape[0]
    projected = jnp.einsum("tnc,cr->tnr", w_qkv, full_x, preferred_element_type=jnp.float32).astype(
        jnp.bfloat16
    )
    query = projected[0]
    packed = jnp.concatenate([projected[1].T, projected[2].T], axis=1)
    padded = jnp.concatenate([packed, jnp.zeros((1, 2 * channels), jnp.bfloat16)], axis=0)
    outgoing = padded[lists]
    pieces = []
    for peer in range(3):
        pieces.append(passed_along(outgoing[peer], "tile", offsets[peer]))
    halo = jnp.stack(pieces)
    extended = jnp.concatenate([packed, halo.reshape(3 * border, 2 * channels)], axis=0)
    grad_att = jnp.dot(w_out, full_dy, preferred_element_type=jnp.float32)
    grad_ext, attended, grad_query = attention(
        extended, neighbors, query, grad_att, min(1024, row_count)
    )
    grad_halo = grad_ext[row_count:].reshape(3, border, 2 * channels)
    answers = []
    for peer in range(3):
        answers.append(passed_along(grad_halo[peer], "tile", (groups - offsets[peer]) % groups))
    backward = jnp.stack(answers)
    own_grad = jnp.concatenate(
        [grad_ext[:row_count], jnp.zeros((1, 2 * channels), jnp.float32)], axis=0
    )
    own_grad = own_grad.at[lists.reshape(-1)].add(backward.reshape(3 * border, 2 * channels))[
        :row_count
    ]
    grad_proj = jnp.stack([grad_query, own_grad[:, :channels].T, own_grad[:, channels:].T]).astype(
        jnp.bfloat16
    )
    grad_scale = 1.0 / math.sqrt(row_count * groups)
    part_qkv = (
        jnp.einsum("tnr,cr->tnc", grad_proj, full_x, preferred_element_type=jnp.float32)
        * grad_scale
    )
    part_out = (
        lax.dot_general(
            attended, full_dy, (((1,), (1,)), ((), ())), preferred_element_type=jnp.float32
        )
        * grad_scale
    )
    grad_qkv, grad_out = lax.psum((part_qkv, part_out), "tile")
    partial_grad = jnp.einsum("tnc,tnr->cr", w_qkv, grad_proj, preferred_element_type=jnp.float32)
    mixed = lax.psum_scatter(partial_grad, "head", scatter_dimension=0, tiled=True)
    d_tokens = mixed + grad_in.astype(jnp.float32)
    return (d_tokens, grad_qkv, grad_out)


def solution(mesh):
    return jax.shard_map(
        local,
        mesh=mesh,
        in_specs=(
            P("head", "tile"),
            P("head", "tile"),
            P(None, "head", None),
            P("head", None),
            P(None, "tile"),
            P("tile", None, None),
        ),
        out_specs=(P("head", "tile"), P(None, "head", None), P("head", None)),
        check_vma=False,
    )
```

profile of v0, /device:TPU:1, one launch (start us, length us, event | category | flops | bytes accessed | tf_op | source)
XLA Modules:
  0.0 895.0 jit_solution(2888538529102410149)
XLA Ops:
  12.4 34.6 %all-gather.3.cloned.1.call-done = bf16[256,4096]{1,0:T(8,128)(2,1)} async-done(((bf16[64,4096]{1,0:T(8,128)(2,1)}), bf16[256,4096]{1,0:T(8,128)(2,1)}) %all-gather.3.cloned.1.call-update) | async-done | bytes 2097168 | tf_op jit(solution)/shard_map/all_gather | solution.py:72
  57.1 25.2 %all-gather.5.cloned.1.call-done = bf16[256,4096]{1,0:T(8,128)(2,1)} async-done(((bf16[64,4096]{1,0:T(8,128)(2,1)}), bf16[256,4096]{1,0:T(8,128)(2,1)}) %all-gather.5.cloned.1.call-update) | async-done | bytes 2097168 | tf_op jit(solution)/shard_map/all_gather | solution.py:73
  88.4 545.0 %while.14 = (s32[]{:T(128)}, f32[4480,128]{1,0:T(8,128)S(1)}, bf16[4,64,1024]{2,1,0:T(8,128)(2,1)}, bf16[4,64,1024]{2,1,0:T(8,128)(2,1)}, s32[4,9,1024]{2,0,1:T(...) while((s32[]{:T(128)}, f32[4480,128]{1,0:T(8,128)S(1)}, ...), condition=%wide.region_4.5_spmd, body=%wide.region_0.4_spmd.sunk | while | flops 11480082 | bytes 107651328 | solution.py:58
  99.4 35.9 %gather_fusion = bf16[9216,128]{1,0:T(8,128)(2,1)} fusion(bf16[4480,128]{1,0:T(8,128)(2,1)S(1)} %get-tuple-element.213, s32[9216]{0:T(1024)} %broadcast_clamp_fusion.2), kind=kCustom, calls=%fused_computation.clone.1 | custom fusion | bytes 4755456 | tf_op jit(solution)/shard_map/while/body/eval_jaxpr/gather | solution.py:31
  135.3 5.3 fusion.49
  140.6 3.8 copy.152
  148.2 3.8 copy.155
  168.1 6.0 copy.158
  174.2 50.6 %scatter_fusion = f32[4480,128]{1,0:T(8,128)S(1)} fusion(f32[4480,128]{1,0:T(8,128)S(1)} %get-tuple-element.200, s32[9216]{0:T(1024)} %bitcast.220, f32[9216,128]{1,0:T(8,128)} %copy.158), kind=kCustom, calls=%fused_computation.2.clone.1 | custom fusion | flops 1179648 | bytes 14192640 | tf_op jit(solution)/shard_map/while/body/eval_jaxpr/scatter-add | solution.py:52
  235.6 35.9 %gather_fusion = bf16[9216,128]{1,0:T(8,128)(2,1)} fusion(bf16[4480,128]{1,0:T(8,128)(2,1)S(1)} %get-tuple-element.213, s32[9216]{0:T(1024)} %broadcast_clamp_fusion.2), kind=kCustom, calls=%fused_computation.clone.1 | custom fusion | bytes 4755456 | tf_op jit(solution)/shard_map/while/body/eval_jaxpr/gather | solution.py:31
  271.5 5.3 fusion.49
  276.8 3.8 copy.152
  284.4 3.8 copy.155
  304.3 6.0 copy.158
  310.3 50.6 %scatter_fusion = f32[4480,128]{1,0:T(8,128)S(1)} fusion(f32[4480,128]{1,0:T(8,128)S(1)} %get-tuple-element.200, s32[9216]{0:T(1024)} %bitcast.220, f32[9216,128]{1,0:T(8,128)} %copy.158), kind=kCustom, calls=%fused_computation.2.clone.1 | custom fusion | flops 1179648 | bytes 14192640 | tf_op jit(solution)/shard_map/while/body/eval_jaxpr/scatter-add | solution.py:52
  371.7 35.9 %gather_fusion = bf16[9216,128]{1,0:T(8,128)(2,1)} fusion(bf16[4480,128]{1,0:T(8,128)(2,1)S(1)} %get-tuple-element.213, s32[9216]{0:T(1024)} %broadcast_clamp_fusion.2), kind=kCustom, calls=%fused_computation.clone.1 | custom fusion | bytes 4755456 | tf_op jit(solution)/shard_map/while/body/eval_jaxpr/gather | solution.py:31
  407.6 5.3 fusion.49
  412.9 3.8 copy.152
  420.5 3.8 copy.155
  440.4 6.0 copy.158
  446.5 50.6 %scatter_fusion = f32[4480,128]{1,0:T(8,128)S(1)} fusion(f32[4480,128]{1,0:T(8,128)S(1)} %get-tuple-element.200, s32[9216]{0:T(1024)} %bitcast.220, f32[9216,128]{1,0:T(8,128)} %copy.158), kind=kCustom, calls=%fused_computation.2.clone.1 | custom fusion | flops 1179648 | bytes 14192640 | tf_op jit(solution)/shard_map/while/body/eval_jaxpr/scatter-add | solution.py:52
  507.8 35.9 %gather_fusion = bf16[9216,128]{1,0:T(8,128)(2,1)} fusion(bf16[4480,128]{1,0:T(8,128)(2,1)S(1)} %get-tuple-element.213, s32[9216]{0:T(1024)} %broadcast_clamp_fusion.2), kind=kCustom, calls=%fused_computation.clone.1 | custom fusion | bytes 4755456 | tf_op jit(solution)/shard_map/while/body/eval_jaxpr/gather | solution.py:31
  543.7 5.3 fusion.49
  549.0 3.8 copy.152
  556.7 3.8 copy.155
  576.6 6.0 copy.158
  582.6 50.6 %scatter_fusion = f32[4480,128]{1,0:T(8,128)S(1)} fusion(f32[4480,128]{1,0:T(8,128)S(1)} %get-tuple-element.200, s32[9216]{0:T(1024)} %bitcast.220, f32[9216,128]{1,0:T(8,128)} %copy.158), kind=kCustom, calls=%fused_computation.2.clone.1 | custom fusion | flops 1179648 | bytes 14192640 | tf_op jit(solution)/shard_map/while/body/eval_jaxpr/scatter-add | solution.py:52
  643.2 3.4 scatter_fusion.1
  648.8 3.8 convolution_bitcast_fusion
  652.6 5.6 copy.88
  665.3 40.3 %reduce-scatter.4.cloned.1.call-done = f32[64,4096]{1,0:T(8,128)} async-done(((f32[256,4096]{1,0:T(8,128)}), f32[64,4096]{1,0:T(8,128)}) %reduce-scatter.4.cloned.1.call-update) | async-done | bytes 1048592
  712.1 173.3 %all-reduce.4.cloned.1.call-done = (f32[3,64,256]{2,1,0:T(8,128)}, f32[64,256]{1,0:T(8,128)}) async-done(((f32[3,64,256]{2,1,0:T(8,128)}, f32[64,256]{1,0:T(8,128)}), (f32[3,64,256]{2,1,0:T(8,128)}, f32[64,256]{1,0:T(8,128)})) %all-reduce.4.cloned.1.call-update) | async-done | bytes 262160 | tf_op jit(solution)/shard_map/psum | solution.py:118
  (244 shorter events, 171.6 us)
Async XLA Ops:
  7.2 39.9 %copy-start = (bf16[3,64,256]{2,1,0:T(8,128)(2,1)S(1)}, bf16[3,64,256]{2,1,0:T(8,128)(2,1)}, u32[]{:S(2)}) copy-start(bf16[3,64,256]{2,1,0:T(8,128)(2,1)} %param.10) | copy-start | bytes 294916
  7.2 39.8 %all-gather.3.cloned.1.call-start = ((), (), s32[]{:S(2)}) async-start(), calls=%async_computation.1 | async-start | bytes 2621440 | tf_op jit(solution)/shard_map/all_gather | solution.py:72
  7.9 74.4 %all-gather.5.cloned.1.call-start = ((), (), s32[]{:S(2)}) async-start(), calls=%async_computation.2 | async-start | bytes 2621440 | tf_op jit(solution)/shard_map/all_gather | solution.py:73
  8.7 696.9 %reduce-scatter.4.cloned.1.call-start = ((), (), s32[]{:S(2)}) async-start(), calls=%async_computation.3 | async-start | bytes 5242880
  50.2 32.1 %copy-start.15 = (bf16[64,256]{1,0:T(8,128)(2,1)S(1)}, bf16[64,256]{1,0:T(8,128)(2,1)}, u32[]{:S(2)}) copy-start(bf16[64,256]{1,0:T(8,128)(2,1)} %param.11) | copy-start | bytes 98308
  52.5 34.3 %collective-permute-start = (bf16[128,128]{1,0:T(8,128)(2,1)S(1)}, bf16[128,128]{1,0:T(8,128)(2,1)S(1)}, u32[]{:S(2)}, u32[]{:S(2)}) collective-permute-start(bf16[128,128]{1,0:T(8,128)(2,1)S(1)} %get-tuple-element.126), channel_id=1, source_target_pairs={{0,4},{4,8},{8,12},{12,16},{16,20},{20,24},{24,28},{28,32},{32,36}... | collective-permute-start | bytes 98312 | tf_op jit(solution)/shard_map/ppermute | solution.py:15
  54.4 32.4 %collective-permute-start.1 = (bf16[128,128]{1,0:T(8,128)(2,1)S(1)}, bf16[128,128]{1,0:T(8,128)(2,1)S(1)}, u32[]{:S(2)}, u32[]{:S(2)}) collective-permute-start(bf16[128,128]{1,0:T(8,128)(2,1)S(1)} %get-tuple-element.127), channel_id=1, source_target_pairs={{0,252},{4,0},{8,4},{12,8},{16,12},{20,16},{24,20},{28,24},{32,28}... | collective-permute-start | bytes 98312 | tf_op jit(solution)/shard_map/ppermute | solution.py:15
  54.4 31.1 %copy-start.9 = (bf16[1,64,4096]{2,1,0:T(8,128)(2,1)S(1)}, bf16[1,64,4096]{2,1,0:T(8,128)(2,1)}, u32[]{:S(2)}) copy-start(bf16[1,64,4096]{2,1,0:T(8,128)(2,1)} %get-tuple-element.121) | copy-start | bytes 1572868
  54.4 32.4 %collective-permute-start.2 = (bf16[128,128]{1,0:T(8,128)(2,1)S(1)}, bf16[128,128]{1,0:T(8,128)(2,1)S(1)}, u32[]{:S(2)}, u32[]{:S(2)}) collective-permute-start(bf16[128,128]{1,0:T(8,128)(2,1)S(1)} %get-tuple-element.128), channel_id=1, source_target_pairs={{0,128},{4,132},{8,136},{12,140},{16,144},{20,148},{24,152},{28,15... | collective-permute-start | bytes 98312 | tf_op jit(solution)/shard_map/ppermute | solution.py:15
  88.4 550.1 %copy-start.17 = (pred[4097]{0:T(1024)(128)(4,1)S(1)}, pred[4097]{0:T(1024)(128)(4,1)}, u32[]{:S(2)}) copy-start(pred[4097]{0:T(1024)(128)(4,1)} %constant.6.clone.1) | copy-start | bytes 12295
  152.0 3.4 copy-start.3
  152.0 4.2 copy-start.1
  153.9 3.4 copy-start.5
  288.2 3.4 copy-start.3
  288.2 4.2 copy-start.1
  290.1 3.4 copy-start.5
  424.4 3.4 copy-start.3
  424.4 4.2 copy-start.1
  426.2 3.3 copy-start.5
  560.5 3.4 copy-start.3
  560.5 4.2 copy-start.1
  562.3 3.4 copy-start.5
  633.4 8.2 copy-start.10
  633.4 9.7 %collective-permute-start.3 = (f32[128,128]{1,0:T(8,128)S(1)}, f32[128,128]{1,0:T(8,128)S(1)}, u32[]{:S(2)}, u32[]{:S(2)}) collective-permute-start(f32[128,128]{1,0:T(8,128)S(1)} %get-tuple-element.118), channel_id=1, source_target_pairs={{0,252},{4,0},{8,4},{12,8},{16,12},{20,16},{24,20},{28,24},{32,28}... | collective-permute-start | bytes 196616 | tf_op jit(solution)/shard_map/ppermute | solution.py:15
  634.2 9.0 %collective-permute-start.5 = (f32[128,128]{1,0:T(8,128)S(1)}, f32[128,128]{1,0:T(8,128)S(1)}, u32[]{:S(2)}, u32[]{:S(2)}) collective-permute-start(f32[128,128]{1,0:T(8,128)S(1)} %get-tuple-element.119), channel_id=1, source_target_pairs={{0,128},{4,132},{8,136},{12,140},{16,144},{20,148},{24,152},{28,15... | collective-permute-start | bytes 196616 | tf_op jit(solution)/shard_map/ppermute | solution.py:15
  636.9 6.3 collective-permute-start.4
  641.6 1.6 copy-start.16
  658.3 3.0 copy-start.7
  658.3 227.1 %all-reduce.4.cloned.1.call-start = ((), (), s32[]{:S(2)}) async-start(), calls=%async_computation.4 | async-start | bytes 524288 | tf_op jit(solution)/shard_map/psum | solution.py:118
  660.0 2.7 copy-start.8
  660.0 2.7 copy-start.11
  660.0 2.7 copy-start.13
  (11 other events, 11.8 us)
Sparse Core Ops, SparseCore 0:
  9.8 37.1 all-gather.2
  48.8 33.4 all-gather.4
  658.4 47.1 reduce-scatter.3
  710.1 175.1 all-reduce.3
where the time goes:
time: 900 us; the launch traced here: 895 us
  local copies, waits for them, and re-layouts  311 us (35%)
  waiting for transfers between devices  275 us (31%)
  other arithmetic  272 us (30%)
  between operations  14.1 us (2%)
  matrix products  12 us (1%)
  starting transfers between devices  9.83 us (1%)
    scatter-add x4, other arithmetic, attend_block(): totals.at[picks.reshape(-1)]  202 us
    psum x1, waiting for transfers between devices, local(): grad_qkv, grad_out = lax.psum((part_qkv, part_out), 'tile')  173 us
    gather x4, local copies, waits for them, and re-layouts, attend_block(): near = extended[picks].astype(jnp.float32)  144 us
    while x72, local copies, waits for them, and re-layouts  59 us
    unnamed x5, waiting for transfers between devices  41.7 us
    all_gather x1, waiting for transfers between devices, local(): lax.all_gather(tokens, 'head', axis=0, tiled=True)  34.6 us
    all_gather x1, waiting for transfers between devices, local(): lax.all_gather(grad_in, 'head', axis=0, tiled=True)  25.2 us
    concatenate x4, local copies, waits for them, and re-layouts, attend_block(): jnp.concatenate([grad_keys.reshape(NBR, block_rows, channels), grad_value...  24.2 us
  transfers between devices with their start and end apart: 10, of which 4 were waited for; matrix products, arithmetic and copies ran while one was open for 4% of the time, Pallas kernels for 0%

commit v1 on v0

--- a/solution.py
+++ b/solution.py
@@ -70,7 +70,9 @@
     lists = send_rows[0]
     full_x, full_dy = (
         lax.all_gather(tokens, "head", axis=0, tiled=True),
-        lax.all_gather(grad_in, "head", axis=0, tiled=True),
+        jnp.concatenate(
+            lax.all_to_all(jnp.stack([grad_in] * lax.axis_size("head")), "head", 0, 0), axis=0
+        ),
     )
     row_count = tokens.shape[1]
     channels = tokens.shape[0]

time: 900 us -> 895 us (level)
  waiting for transfers between devices: 275 us -> 254 us
  local copies, waits for them, and re-layouts: 311 us -> 321 us
    all_to_all x0 -> x1, waiting for transfers between devices: none -> 32.4 us  [local(): lax.all_to_all(jnp.stack([grad_in] * lax.axis_size('head')), 'head', 0, 0)]
    all_gather x1, waiting for transfers between devices: 34.6 us -> 7.13 us  [local(): lax.all_gather(tokens, 'head', axis=0, tiled=True)]
    all_gather x1 -> x0, waiting for transfers between devices: 25.2 us -> none  [local(): lax.all_gather(grad_in, 'head', axis=0, tiled=True)]
    unnamed x33 -> x39, local copies, waits for them, and re-layouts: 17 us -> 18.8 us
    unnamed x5 -> x4, waiting for transfers between devices: 41.7 us -> 40.8 us
  transfers between devices with their start and end apart: 10 -> 10, of which waited for: 4 -> 4; matrix products, arithmetic and copies ran while one was open for 4% -> 3% of each run, Pallas kernels for 0% -> 0%
where the time goes in v1:
time: 895 us; the launch traced here: 890 us
  local copies, waits for them, and re-layouts  321 us (36%)
  other arithmetic  271 us (30%)
  waiting for transfers between devices  254 us (28%)
  starting transfers between devices  16.9 us (2%)
  between operations  14 us (2%)
  matrix products  11.6 us (1%)
    scatter-add x4, other arithmetic, attend_block(): totals.at[picks.reshape(-1)]  202 us
    psum x1, waiting for transfers between devices, local(): grad_qkv, grad_out = lax.psum((part_qkv, part_out), 'tile')  174 us
    gather x4, local copies, waits for them, and re-layouts, attend_block(): near = extended[picks].astype(jnp.float32)  144 us
    while x72, local copies, waits for them, and re-layouts  59 us
    unnamed x4, waiting for transfers between devices  40.8 us
    all_to_all x1, waiting for transfers between devices, local(): lax.all_to_all(jnp.stack([grad_in] * lax.axis_size('head')), 'head', 0, 0)  32.4 us
    concatenate x4, local copies, waits for them, and re-layouts, attend_block(): jnp.concatenate([grad_keys.reshape(NBR, block_rows, channels), grad_value...  24.2 us
    slice x4, local copies, waits for them, and re-layouts, attend_block(): near[:, :, channels:].reshape(NBR, block_rows, local_heads, head_dim)  21.2 us
  transfers between devices with their start and end apart: 10, of which 4 were waited for; matrix products, arithmetic and copies ran while one was open for 3% of the time, Pallas kernels for 0%

profile of v1, /device:TPU:1, one launch (start us, length us, event | category | flops | bytes accessed | tf_op | source)
XLA Modules:
  0.0 890.0 jit_solution(11420758721417508965)
XLA Ops:
  10.5 5.0 all-to-all-start
  16.9 32.4 %all-to-all-done = bf16[4,64,4096]{2,1,0:T(8,128)(2,1)S(1)} async-done(((bf16[4,64,4096]{2,1,0:T(8,128)(2,1)}), bf16[4,64,4096]{2,1,0:T(8,128)(2,1)S(1)}, u32[]{:S(2)}, u32[]{:S(2)}) %all-to-all-start) | async-done | bytes 2097184 | tf_op jit(solution)/shard_map/all_to_all | solution.py:74
  52.2 7.1 all-gather.2.cloned.1.call-done
  81.4 545.1 %while.14 = (s32[]{:T(128)}, f32[4480,128]{1,0:T(8,128)S(1)}, bf16[4,64,1024]{2,1,0:T(8,128)(2,1)}, bf16[4,64,1024]{2,1,0:T(8,128)(2,1)}, s32[4,9,1024]{2,0,1:T(...) while((s32[]{:T(128)}, f32[4480,128]{1,0:T(8,128)S(1)}, ...), condition=%wide.region_4.5_spmd, body=%wide.region_0.4_spmd.sunk | while | flops 11480082 | bytes 107651328 | solution.py:58
  92.4 35.9 %gather_fusion = bf16[9216,128]{1,0:T(8,128)(2,1)} fusion(bf16[4480,128]{1,0:T(8,128)(2,1)S(1)} %get-tuple-element.213, s32[9216]{0:T(1024)} %broadcast_clamp_fusion.2), kind=kCustom, calls=%fused_computation.clone.1 | custom fusion | bytes 4755456 | tf_op jit(solution)/shard_map/while/body/eval_jaxpr/gather | solution.py:31
  128.3 5.3 fusion.48
  133.6 3.8 copy.150
  141.2 3.8 copy.153
  161.1 6.0 copy.156
  167.2 50.6 %scatter_fusion = f32[4480,128]{1,0:T(8,128)S(1)} fusion(f32[4480,128]{1,0:T(8,128)S(1)} %get-tuple-element.200, s32[9216]{0:T(1024)} %bitcast.222, f32[9216,128]{1,0:T(8,128)} %copy.156), kind=kCustom, calls=%fused_computation.2.clone.1 | custom fusion | flops 1179648 | bytes 14192640 | tf_op jit(solution)/shard_map/while/body/eval_jaxpr/scatter-add | solution.py:52
  228.6 35.9 %gather_fusion = bf16[9216,128]{1,0:T(8,128)(2,1)} fusion(bf16[4480,128]{1,0:T(8,128)(2,1)S(1)} %get-tuple-element.213, s32[9216]{0:T(1024)} %broadcast_clamp_fusion.2), kind=kCustom, calls=%fused_computation.clone.1 | custom fusion | bytes 4755456 | tf_op jit(solution)/shard_map/while/body/eval_jaxpr/gather | solution.py:31
  264.5 5.3 fusion.48
  269.8 3.8 copy.150
  277.4 3.8 copy.153
  297.3 6.0 copy.156
  303.4 50.6 %scatter_fusion = f32[4480,128]{1,0:T(8,128)S(1)} fusion(f32[4480,128]{1,0:T(8,128)S(1)} %get-tuple-element.200, s32[9216]{0:T(1024)} %bitcast.222, f32[9216,128]{1,0:T(8,128)} %copy.156), kind=kCustom, calls=%fused_computation.2.clone.1 | custom fusion | flops 1179648 | bytes 14192640 | tf_op jit(solution)/shard_map/while/body/eval_jaxpr/scatter-add | solution.py:52
  364.8 35.9 %gather_fusion = bf16[9216,128]{1,0:T(8,128)(2,1)} fusion(bf16[4480,128]{1,0:T(8,128)(2,1)S(1)} %get-tuple-element.213, s32[9216]{0:T(1024)} %broadcast_clamp_fusion.2), kind=kCustom, calls=%fused_computation.clone.1 | custom fusion | bytes 4755456 | tf_op jit(solution)/shard_map/while/body/eval_jaxpr/gather | solution.py:31
  400.7 5.3 fusion.48
  406.0 3.8 copy.150
  413.6 3.8 copy.153
  433.5 6.0 copy.156
  439.5 50.6 %scatter_fusion = f32[4480,128]{1,0:T(8,128)S(1)} fusion(f32[4480,128]{1,0:T(8,128)S(1)} %get-tuple-element.200, s32[9216]{0:T(1024)} %bitcast.222, f32[9216,128]{1,0:T(8,128)} %copy.156), kind=kCustom, calls=%fused_computation.2.clone.1 | custom fusion | flops 1179648 | bytes 14192640 | tf_op jit(solution)/shard_map/while/body/eval_jaxpr/scatter-add | solution.py:52
  500.9 35.9 %gather_fusion = bf16[9216,128]{1,0:T(8,128)(2,1)} fusion(bf16[4480,128]{1,0:T(8,128)(2,1)S(1)} %get-tuple-element.213, s32[9216]{0:T(1024)} %broadcast_clamp_fusion.2), kind=kCustom, calls=%fused_computation.clone.1 | custom fusion | bytes 4755456 | tf_op jit(solution)/shard_map/while/body/eval_jaxpr/gather | solution.py:31
  536.9 5.3 fusion.48
  542.2 3.8 copy.150
  549.8 3.8 copy.153
  569.7 6.0 copy.156
  575.7 50.6 %scatter_fusion = f32[4480,128]{1,0:T(8,128)S(1)} fusion(f32[4480,128]{1,0:T(8,128)S(1)} %get-tuple-element.200, s32[9216]{0:T(1024)} %bitcast.222, f32[9216,128]{1,0:T(8,128)} %copy.156), kind=kCustom, calls=%fused_computation.2.clone.1 | custom fusion | flops 1179648 | bytes 14192640 | tf_op jit(solution)/shard_map/while/body/eval_jaxpr/scatter-add | solution.py:52
  626.5 4.9 collective-permute-start.3
  647.6 5.6 copy.89
  660.2 40.1 %reduce-scatter.4.cloned.1.call-done = f32[64,4096]{1,0:T(8,128)} async-done(((f32[256,4096]{1,0:T(8,128)}), f32[64,4096]{1,0:T(8,128)}) %reduce-scatter.4.cloned.1.call-update) | async-done | bytes 1048592
  706.8 173.6 %all-reduce.4.cloned.1.call-done = (f32[3,64,256]{2,1,0:T(8,128)}, f32[64,256]{1,0:T(8,128)}) async-done(((f32[3,64,256]{2,1,0:T(8,128)}, f32[64,256]{1,0:T(8,128)}), (f32[3,64,256]{2,1,0:T(8,128)}, f32[64,256]{1,0:T(8,128)})) %all-reduce.4.cloned.1.call-update) | async-done | bytes 262160 | tf_op jit(solution)/shard_map/psum | solution.py:120
  (250 shorter events, 184.1 us)
Async XLA Ops:
  7.2 52.1 %copy-start = (bf16[3,64,256]{2,1,0:T(8,128)(2,1)S(1)}, bf16[3,64,256]{2,1,0:T(8,128)(2,1)}, u32[]{:S(2)}) copy-start(bf16[3,64,256]{2,1,0:T(8,128)(2,1)} %param.10) | copy-start | bytes 294916
  7.2 52.1 %all-gather.2.cloned.1.call-start = ((), (), s32[]{:S(2)}) async-start(), calls=%async_computation.2 | async-start | bytes 2621440 | tf_op jit(solution)/shard_map/all_gather | solution.py:72
  10.5 5.0 copy-start.16
  10.5 5.8 copy-start.19
  10.5 38.8 %all-to-all-start = ((bf16[4,64,4096]{2,1,0:T(8,128)(2,1)}), bf16[4,64,4096]{2,1,0:T(8,128)(2,1)S(1)}, u32[]{:S(2)}, u32[]{:S(2)}) async-start(bf16[4,64,4096]{2,1,0:T(8,128)(2,1)} %stack.47), calls=%async_computation | async-start | bytes 4194304 | tf_op jit(solution)/shard_map/all_to_all | solution.py:74
  15.5 684.8 %reduce-scatter.4.cloned.1.call-start = ((), (), s32[]{:S(2)}) async-start(), calls=%async_computation.3 | async-start | bytes 5242880
  49.3 12.2 %copy-start.6 = (bf16[4,64,4096]{2,1,0:T(8,128)(2,1)}, bf16[4,64,4096]{2,1,0:T(8,128)(2,1)S(1)}, u32[]{:S(2)}) copy-start(bf16[4,64,4096]{2,1,0:T(8,128)(2,1)S(1)} %all-to-all-done) | copy-start | bytes 6291460
  63.5 12.2 %copy-start.9 = (bf16[4096,256]{1,0:T(8,128)(2,1)S(1)}, bf16[4096,256]{1,0:T(8,128)(2,1)}, u32[]{:S(2)}) copy-start(bf16[4096,256]{1,0:T(8,128)(2,1)} %copy.53) | copy-start | bytes 6291460
  63.5 12.2 %copy-start.17 = (bf16[64,256]{1,0:T(8,128)(2,1)S(1)}, bf16[64,256]{1,0:T(8,128)(2,1)}, u32[]{:S(2)}) copy-start(bf16[64,256]{1,0:T(8,128)(2,1)} %param.11) | copy-start | bytes 98308
  70.7 9.1 %collective-permute-start = (bf16[128,128]{1,0:T(8,128)(2,1)S(1)}, bf16[128,128]{1,0:T(8,128)(2,1)S(1)}, u32[]{:S(2)}, u32[]{:S(2)}) collective-permute-start(bf16[128,128]{1,0:T(8,128)(2,1)S(1)} %get-tuple-element.126), channel_id=1, source_target_pairs={{0,4},{4,8},{8,12},{12,16},{16,20},{20,24},{24,28},{28,32},{32,36}... | collective-permute-start | bytes 98312 | tf_op jit(solution)/shard_map/ppermute | solution.py:15
  72.8 7.1 collective-permute-start.1
  72.8 7.1 collective-permute-start.2
  81.4 552.1 %copy-start.20 = (pred[4097]{0:T(1024)(128)(4,1)S(1)}, pred[4097]{0:T(1024)(128)(4,1)}, u32[]{:S(2)}) copy-start(pred[4097]{0:T(1024)(128)(4,1)} %constant.6.clone.1) | copy-start | bytes 12295
  145.1 3.4 copy-start.3
  145.1 4.2 copy-start.1
  146.9 3.4 copy-start.5
  281.2 3.4 copy-start.3
  281.2 4.2 copy-start.1
  283.1 3.4 copy-start.5
  417.4 3.4 copy-start.3
  417.4 4.2 copy-start.1
  419.3 3.3 copy-start.5
  553.6 3.4 copy-start.3
  553.6 4.2 copy-start.1
  555.5 3.4 copy-start.5
  626.5 10.1 %copy-start.11 = (bf16[4,64,1024]{2,1,0:T(8,128)(2,1)S(1)}, bf16[4,64,1024]{2,1,0:T(8,128)(2,1)}, u32[]{:S(2)}) copy-start(bf16[4,64,1024]{2,1,0:T(8,128)(2,1)} %get-tuple-element.47) | copy-start | bytes 1572868
  626.5 11.6 %collective-permute-start.3 = (f32[128,128]{1,0:T(8,128)S(1)}, f32[128,128]{1,0:T(8,128)S(1)}, u32[]{:S(2)}, u32[]{:S(2)}) collective-permute-start(f32[128,128]{1,0:T(8,128)S(1)} %get-tuple-element.118), channel_id=1, source_target_pairs={{0,252},{4,0},{8,4},{12,8},{16,12},{20,16},{24,20},{28,24},{32,28}... | collective-permute-start | bytes 196616 | tf_op jit(solution)/shard_map/ppermute | solution.py:15
  631.5 6.7 collective-permute-start.5
  633.4 4.7 collective-permute-start.4
  653.2 3.0 copy-start.7
  653.2 227.1 %all-reduce.4.cloned.1.call-start = ((), (), s32[]{:S(2)}) async-start(), calls=%async_computation.4 | async-start | bytes 524288 | tf_op jit(solution)/shard_map/psum | solution.py:120
  655.0 2.7 copy-start.10
  (14 other events, 18.8 us)
Sparse Core Ops, SparseCore 0:
  9.8 49.4 all-gather.1
  653.4 46.9 reduce-scatter.3
  705.0 175.3 all-reduce.3
